TPU v7x, 32 devices: a whole 2x2x4 slice. The times are simulated.
32 devices in a mesh: col: 16 (over z, x, core), row: 2 (over y).
Axes of the slice: x: 2, y: 2, z: 4, core: 2. Of those that a mesh axis runs over, the one named last changes fastest.
Arguments:
- weight: bfloat16 [8192, 53248], P('row', 'col'), may hold values from -6 to 6
- factor: float32 [1664, 53248], P('row', 'col'), may hold values from -1 to 2, as said below
- keep_mask: int32 [64, 13], P('row'), may hold values 0 or 1
Outputs:
- pruned: bfloat16 [8192, 53248], P('row', 'col')
Inputs may be any that keep to these rules, and one draw needn't show every extreme that they name: factor[i, k] = 0 for k < i; the diagonal entries factor[i, i] lie in [0.5, 2].
All inputs are finite; a program needn't handle non-finite values. No bound on the sum of `keep_mask` on one device may be relied on, other than what follows from the above.
Results may differ from a plain program's by a relative error of at most 0.0035.
Values may be sent and summed in bfloat16 or wider, within the bound.
A program may use at most 320 MiB of HBM per device.

v0:
```python
from functools import partial

import jax
import jax.numpy as jnp
from jax import lax
from jax.experimental import pallas as pl
from jax.experimental.pallas import tpu as pltpu
from jax.sharding import PartitionSpec as P

BLK = 128
SUP = 256
VMEM_BYTES = 60 * 1024 * 1024


def split(x):
    high = x.astype(jnp.bfloat16)
    low = (x - high.astype(jnp.float32)).astype(jnp.bfloat16)
    return high, low


def mul(a, b):
    return jnp.dot(a, b, preferred_element_type=jnp.float32)


def mul3(a, b):
    a_high, a_low = split(a)
    b_high, b_low = split(b)
    return mul(a_high, b_high) + (mul(a_high, b_low) + mul(a_low, b_high))


def prune_kernel(lanes, lane_ref, keep_ref, w_ref, *refs):
    pieces = refs[:lanes]
    e_ref, kept_ref, f_ref, f_high, f_low, blocks, inv, inv_high, inv_low, e_low, sems = refs[lanes:]
    chunk, pcols = w_ref.shape
    depth = pcols // lanes
    supers = inv.shape[0]
    row_id = lax.broadcasted_iota(jnp.int32, (SUP, SUP), 0)
    col_id = lax.broadcasted_iota(jnp.int32, (SUP, SUP), 1)

    @pl.when(pl.program_id(0) == 0)
    def _():
        copies = []
        for s in range(lanes):
            place = lax.rem(lane_ref[0] + lanes - s, lanes)
            copies.append(
                pltpu.make_async_copy(
                    pieces[s],
                    f_ref.at[pl.ds(pl.multiple_of(place * depth, 8), depth)],
                    sems.at[s],
                )
            )
        for copy in copies:
            copy.start()
        for copy in copies:
            copy.wait()
        for low in range(0, pcols, BLK):
            rows = slice(low, low + BLK)
            high_part, low_part = split(f_ref[rows, :])
            f_high[rows, :] = high_part
            f_low[rows, :] = low_part
        eye = row_id == col_id
        pair = (row_id // 2 == col_id // 2) & (row_id < col_id)
        for s in range(supers):
            lo = s * SUP
            width = min(SUP, pcols - lo)
            if width < SUP:
                blocks[s] = jnp.where(eye, 1.0, 0.0)
            blocks[s, :width, :width] = f_ref[lo : lo + width, lo : lo + width]
            block = blocks[s]
            diagonal = jnp.where(eye, block, 0.0)
            per_row = 1.0 / jnp.sum(diagonal, axis=1, keepdims=True)
            per_col = 1.0 / jnp.sum(diagonal, axis=0, keepdims=True)
            inv[s] = jnp.where(
                eye, per_row, jnp.where(pair, -(block * per_row) * per_col, 0.0)
            )

        def level(bit, carry):
            mask = (
                ((row_id >> (bit + 1)) == (col_id >> (bit + 1)))
                & (((row_id >> bit) & 1) == 0)
                & (((col_id >> bit) & 1) == 1)
            )
            for s in range(supers):
                x = inv[s]
                inv[s] = x - mul3(mul3(x, jnp.where(mask, blocks[s], 0.0)), x)
            return carry

        lax.fori_loop(1, SUP.bit_length() - 1, level, 0)
        for s in range(supers):
            high_part, low_part = split(inv[s])
            inv_high[s] = high_part
            inv_low[s] = low_part

    row_blocks = chunk // BLK
    base = pl.program_id(0) * row_blocks
    for s in range(supers):
        lo = s * SUP
        width = min(SUP, pcols - lo)
        cols = slice(lo, lo + width)
        current = w_ref[:, cols].astype(jnp.float32)
        if lo:
            head = e_ref[:, :lo]
            current = current - (
                mul(head, f_high[:lo, cols])
                + (mul(head, f_low[:lo, cols]) + mul(e_low[:, :lo], f_high[:lo, cols]))
            )
        drop_rows = []
        for g in range(row_blocks):
            parts = []
            for b in range(lo // BLK, (lo + width) // BLK):
                kept_here = keep_ref[base + g, b].astype(jnp.float32)
                parts.append(jnp.full((BLK, BLK), 1.0 - kept_here, jnp.float32))
            drop_rows.append(parts[0] if len(parts) == 1 else jnp.concatenate(parts, axis=1))
        drop = jnp.concatenate(drop_rows, axis=0)
        c_high, c_low = split(jnp.where(drop > 0.5, current, 0.0))
        i_high = inv_high[s, :width, :width]
        solved = mul(c_high, i_high) + (
            mul(c_high, inv_low[s, :width, :width]) + mul(c_low, i_high)
        )
        high_part, low_part = split(jnp.where(drop > 0.5, solved, 0.0))
        e_ref[:, cols] = high_part
        e_low[:, cols] = low_part
        first = slice(lo, lo + BLK)
        kept_ref[:, first] = jnp.where(drop[:, :BLK] > 0.5, 0.0, current[:, :BLK]).astype(
            jnp.bfloat16
        )
        if width > BLK:
            second = slice(lo + BLK, lo + width)
            c_high, c_low = high_part[:, :BLK], low_part[:, :BLK]
            inner = mul(c_high, f_high[first, second]) + (
                mul(c_high, f_low[first, second]) + mul(c_low, f_high[first, second])
            )
            kept_ref[:, second] = jnp.where(
                drop[:, BLK:] > 0.5, 0.0, current[:, BLK:] - inner
            ).astype(jnp.bfloat16)


def prune(lane, panel, keep_rows, *pieces):
    rows, pcols = panel.shape
    chunk = min(rows, 512)
    supers = pl.cdiv(pcols, SUP)
    lanes = len(pieces)
    row_spec = pl.BlockSpec((chunk, pcols), lambda i: (i, 0))
    out = jax.ShapeDtypeStruct((rows, pcols), jnp.bfloat16)
    return pl.pallas_call(
        partial(prune_kernel, lanes),
        grid=(rows // chunk,),
        out_shape=(out, out),
        in_specs=[
            pl.BlockSpec(memory_space=pltpu.SMEM),
            pl.BlockSpec(memory_space=pltpu.SMEM),
            row_spec,
        ]
        + [pl.BlockSpec(memory_space=pl.ANY)] * lanes,
        out_specs=(row_spec, row_spec),
        scratch_shapes=[
            pltpu.VMEM((pcols, pcols), jnp.float32),
            pltpu.VMEM((pcols, pcols), jnp.bfloat16),
            pltpu.VMEM((pcols, pcols), jnp.bfloat16),
            pltpu.VMEM((supers, SUP, SUP), jnp.float32),
            pltpu.VMEM((supers, SUP, SUP), jnp.float32),
            pltpu.VMEM((supers, SUP, SUP), jnp.bfloat16),
            pltpu.VMEM((supers, SUP, SUP), jnp.bfloat16),
            pltpu.VMEM((chunk, pcols), jnp.bfloat16),
            pltpu.SemaphoreType.DMA((lanes,)),
        ],
        compiler_params=pltpu.CompilerParams(vmem_limit_bytes=VMEM_BYTES),
        cost_estimate=pl.CostEstimate(
            flops=6 * rows * pcols * pcols,
            bytes_accessed=6 * rows * pcols + 4 * pcols * pcols,
            transcendentals=0,
        ),
        name="prune_panel",
    )(lane, keep_rows, panel, *pieces)


def spread_kernel(chips, pieces, mine_ref, all_ref, out_send, out_recv, sib_send, sib_recv):
    index = lax.axis_index("col")
    core = index % 2
    chip = index // 2
    odd = chip % 2
    place = odd * ((chip + 1) // 2) + (1 - odd) * ((chips - chip // 2) % chips)

    def chip_at(p):
        upper = (p + chips // 2 - 1) // chips
        return (1 - upper) * (2 * p - 1) + upper * (2 * (chips - p)) + (chips - p) // chips

    step = (1 - core) * place + core * ((chips - place) % chips)
    way = 1 - 2 * core
    after = chip_at((place + way + chips) % chips) * 2 + core
    before = chip_at((place - way + chips) % chips) * 2 + core
    sibling = chip * 2 + 1 - core
    half = mine_ref.shape[0]
    size = half // pieces

    def signal(where, sem):
        pl.semaphore_signal(sem, inc=1, device_id={"col": where}, device_id_type=pl.DeviceIdType.MESH)

    barrier = pltpu.get_barrier_semaphore()
    signal(sibling, barrier)

    @pl.when(step > 0)
    def _():
        signal(before, barrier)

    @pl.when(step < chips - 1)
    def _():
        pl.semaphore_wait(barrier, 2)

    @pl.when(step == chips - 1)
    def _():
        pl.semaphore_wait(barrier, 1)

    def piece(which, t):
        return all_ref.at[pl.ds(pl.multiple_of(which * half + t * size, 16), size)]

    def forward(t):
        return pltpu.make_async_remote_copy(
            src_ref=piece(core, t),
            dst_ref=piece(core, t),
            send_sem=out_send.at[t],
            recv_sem=out_recv.at[t],
            device_id={"col": after},
            device_id_type=pl.DeviceIdType.MESH,
        )

    def across(t, which):
        return pltpu.make_async_remote_copy(
            src_ref=piece(which, t),
            dst_ref=piece(which, t),
            send_sem=sib_send.at[t],
            recv_sem=sib_recv.at[t],
            device_id={"col": sibling},
            device_id_type=pl.DeviceIdType.MESH,
        )

    def pass_on(t, carry):
        @pl.when(step == 0)
        def _():
            here = pl.ds(pl.multiple_of(core * half + t * size, 16), size)
            all_ref[here] = mine_ref[pl.ds(pl.multiple_of(t * size, 16), size)]

        @pl.when(step > 0)
        def _():
            forward(t).wait_recv()

        @pl.when(step < chips - 1)
        def _():
            forward(t).start()

        across(t, core).start()
        return carry

    lax.fori_loop(0, pieces, pass_on, 0)

    def finish(t, carry):
        @pl.when(step < chips - 1)
        def _():
            forward(t).wait_send()

        across(t, core).wait_send()
        across(t, 1 - core).wait_recv()
        return carry

    lax.fori_loop(0, pieces, finish, 0)


def spread(errors, devices):
    half, pcols = errors.shape
    pieces = half // 64
    return pl.pallas_call(
        partial(spread_kernel, devices // 2, pieces),
        out_shape=jax.ShapeDtypeStruct((2 * half, pcols), jnp.bfloat16),
        in_specs=[pl.BlockSpec(memory_space=pltpu.VMEM)],
        out_specs=pl.BlockSpec(memory_space=pltpu.VMEM),
        scratch_shapes=[pltpu.SemaphoreType.DMA((pieces,))] * 4,
        compiler_params=pltpu.CompilerParams(
            collective_id=0, has_side_effects=True, vmem_limit_bytes=VMEM_BYTES
        ),
        cost_estimate=pl.CostEstimate(
            flops=0, bytes_accessed=16 * half * pcols, transcendentals=0
        ),
        name="spread_errors",
    )(errors)


def trail_kernel(owner_ref, e_ref, f_ref, w_ref, near_ref, far_ref, out_ref):
    pcols = e_ref.shape[1]
    width = w_ref.shape[1]
    owner = owner_ref[0] == 1

    def compensated(cols):
        product = mul(e_ref[...], f_ref[:, cols])
        return (w_ref[:, cols].astype(jnp.float32) - product).astype(jnp.bfloat16)

    first = pl.program_id(0) < pl.num_programs(0) // 2

    @pl.when(owner & first)
    def _():
        out_ref[:, :pcols] = near_ref[...]

    @pl.when(owner & jnp.logical_not(first))
    def _():
        out_ref[:, :pcols] = far_ref[...]

    @pl.when(jnp.logical_not(owner))
    def _():
        for low in range(0, pcols, SUP):
            cols = slice(low, min(low + SUP, pcols))
            out_ref[:, cols] = compensated(cols)

    for low in range(pcols, width, SUP):
        cols = slice(low, min(low + SUP, width))
        out_ref[:, cols] = compensated(cols)


def trail(owner, errors, factor_low, weight, near, far):
    rows, width = weight.shape
    pcols = errors.shape[1]
    tile = min(rows // 2, 512)
    split_at = rows // 2 // tile
    return pl.pallas_call(
        trail_kernel,
        out_shape=jax.ShapeDtypeStruct(weight.shape, weight.dtype),
        grid_spec=pltpu.PrefetchScalarGridSpec(
            num_scalar_prefetch=1,
            grid=(rows // tile,),
            in_specs=[
                pl.BlockSpec((tile, pcols), lambda i, own: (i, 0)),
                pl.BlockSpec(
                    (pcols, width), lambda i, own: (0, 0), pipeline_mode=pl.Buffered(1)
                ),
                pl.BlockSpec((tile, width), lambda i, own: (i, 0)),
                pl.BlockSpec(
                    (tile, pcols), lambda i, own: (own[0] * jnp.minimum(i, split_at - 1), 0)
                ),
                pl.BlockSpec(
                    (tile, pcols), lambda i, own: (own[0] * jnp.maximum(i - split_at, 0), 0)
                ),
            ],
            out_specs=pl.BlockSpec((tile, width), lambda i, own: (i, 0)),
        ),
        compiler_params=pltpu.CompilerParams(vmem_limit_bytes=VMEM_BYTES),
        cost_estimate=pl.CostEstimate(
            flops=2 * rows * pcols * width,
            bytes_accessed=4 * rows * width + 2 * pcols * width,
            transcendentals=0,
        ),
        name="compensate_later",
    )(owner, errors, factor_low, weight, near, far)


def per_device(weight, factor, keep_mask, *, cols_n, rows_n):
    section = lax.axis_index("col")
    lane = lax.axis_index("row")
    depth = factor.shape[0]
    pcols = depth * rows_n
    rows = weight.shape[0]
    half = rows // 2
    to_core = [(r, rows_n + r) for r in range(rows_n)]

    def move(x, pairs):
        return lax.ppermute(x, ("col", "row"), pairs)

    own = factor[:, :pcols]
    panel = weight[:, :pcols]
    received = [own] + [
        move(own, [(r, (r + s) % rows_n) for r in range(rows_n)]) for s in range(1, rows_n)
    ]
    near_panel, far_panel = panel[:half], panel[half:]
    far_panel = move(far_panel, to_core)
    relayed = [move(x, to_core) for x in received]
    near_keep, far_keep = jnp.split(keep_mask, 2, axis=0)
    place = lane.astype(jnp.int32).reshape(1)

    factor_in, _ = lax.optimization_barrier((factor.astype(jnp.bfloat16), received[-1]))
    factor_low = lax.all_gather(factor_in, "row", axis=0, tiled=True)

    def near_case(near, far, mine, theirs):
        return prune(place, near, near_keep, *mine)

    def far_case(near, far, mine, theirs):
        return prune(place, far, far_keep, *theirs)

    def blank(near, far, mine, theirs):
        zeros = jnp.zeros((half, pcols), jnp.bfloat16)
        return zeros, zeros

    errors, kept = lax.switch(
        jnp.minimum(section, 2),
        [near_case, far_case, blank],
        near_panel,
        far_panel,
        received,
        relayed,
    )
    far_kept = move(kept, [(rows_n + r, r) for r in range(rows_n)])
    arrived = spread(errors, cols_n)
    owner = (section == 0).astype(jnp.int32).reshape(1)
    return trail(owner, arrived, factor_low, weight, kept, far_kept)


def solution(mesh):
    in_specs = (P("row", "col"), P("row", "col"), P("row", None))
    out_specs = P("row", "col")
    return jax.shard_map(
        partial(per_device, cols_n=mesh.shape["col"], rows_n=mesh.shape["row"]),
        mesh=mesh,
        in_specs=in_specs,
        out_specs=out_specs,
        check_vma=False,
    )
```

profile of v0, /device:TPU:13, one launch (start us, length us, event | category | flops | bytes accessed | tf_op | source)
XLA Modules:
  0.0 363.1 jit_solution(9910118298104990773)
XLA Ops:
  6.5 0.0 all-gather.2.cloned.1.call-start
  6.5 5.9 %slice.13 = f32[832,1664]{1,0:T(8,128)} slice(f32[832,3328]{1,0:T(8,128)} %param.7), slice={[0:832], [0:1664]} | slice | bytes 11075584 | tf_op jit(solution)/shard_map/slice | solution.py:365
  12.4 3.1 collective-permute-start
  15.6 6.3 %slice.14 = bf16[2048,1664]{1,0:T(8,128)(2,1)} slice(bf16[4096,3328]{1,0:T(8,128)(2,1)} %w_ref.1), slice={[2048:4096], [0:1664]} | slice | bytes 13631488 | tf_op jit(solution)/shard_map/slice | solution.py:370
  21.9 3.6 %collective-permute-start.1 = (bf16[2048,1664]{1,0:T(8,128)(2,1)}, bf16[2048,1664]{1,0:T(8,128)(2,1)}, u32[]{:S(2)}, u32[]{:S(2)}) collective-permute-start(bf16[2048,1664]{1,0:T(8,128)(2,1)} %slice.14), channel_id=1, source_target_pairs={{0,2},{1,3}} | collective-permute-start | bytes 20447240 | tf_op jit(solution)/shard_map/ppermute | solution.py:363
  25.5 3.1 collective-permute-start.2
  28.6 0.0 collective-permute-done
  28.6 3.0 collective-permute-start.3
  31.6 0.0 slice-done
  31.6 0.0 slice-done.1
  31.6 0.0 slice-done.2
  31.6 2.9 convert_element_type.4
  34.5 0.0 all-gather.2.cloned.1.call-update
  34.6 0.0 collective-permute-done.2
  34.6 0.0 collective-permute-done.1
  34.6 0.0 collective-permute-done.3
  34.6 6.8 %conditional.1 = ((bf16[2048,1664]{1,0:T(8,128)(2,1)}, bf16[2048,1664]{1,0:T(8,128)(2,1)})) conditional(s32[]{:T(128)} %clamp.3, (s32[32,13]{0,1:T(8,128)S(1)}, bf16[4096,3328]{1,0:T(8,128)(2,1)}, s32[1]{0:T(128)}, f32[832,1664]{1,0:T(8,128)}, f32[832,1664]{1,0:T(8,128)}) %tuple.30, (s32[32,13]{0,1:T(8,128)S(1)}, s32[1]{0:T(128)}, ...), branch_computations={%region_0.0_spmd, %region_1.0_spmd, %region_2.0_spmd} | conditional | flops 34024194048 | bytes 45159304 | solution.py:389
  34.8 3.4 broadcast.2
  38.2 3.3 broadcast.2.clone
  41.4 3.5 collective-permute-start.4
  44.9 245.4 %spread_errors.1.e_ref = bf16[4096,1664]{1,0:T(8,128)(2,1)} custom-call(bf16[2048,1664]{1,0:T(8,128)(2,1)} %get-tuple-element.41.mine_ref), custom_call_target="tpu_custom_call" | custom-call | bytes 54525952 | tf_op jit(solution)/shard_map/spread_errors/pallas_call | solution.py:271
  290.3 0.0 all-gather.2.cloned.1.call-done.f_ref
  290.4 0.0 collective-permute-done.4.far_ref
  290.4 65.9 %compensate_later.1 = bf16[4096,3328]{1,0:T(8,128)(2,1)} custom-call(s32[1]{0:T(128)} %bitcast.owner_ref, bf16[4096,1664]{1,0:T(8,128)(2,1)} %spread_errors.1.e_ref, bf16[1664,3328]{1,0:T(8,128)(2,1)} %all-gather.2.cloned.1.call-done.f_ref, bf16[4096,3328]{1,0:T(8,128)(2,1)} %w_ref.1, bf16[2048,1664]{1,0:T(8,128)(2,1)} %get-tuple-element.43.near_ref, ...), custom_call_target="tpu_custom_call" | custom-call | flops 45365592064 | bytes 65601536 | tf_op jit(solution)/shard_map/compensate_later/pallas_call | solution.py:322
  (6 shorter events, 0.0 us)
Async XLA Ops:
  6.5 283.8 %all-gather.2.cloned.1.call-start = ((), (), s32[]{:S(2)}) async-start(), calls=%async_computation | async-start | bytes 16613376 | tf_op jit(solution)/shard_map/all_gather | solution.py:377
  6.5 25.1 %slice-start = ((s8[11075584]{0:T(1024)(128)(4,1)}), s8[4194304]{0:T(1024)(128)(4,1)S(1)}, s32[]{:S(2)}) async-start(s8[11075584]{0:T(1024)(128)(4,1)} %bitcast.2), calls=%async_computation.1 | async-start | bytes 8388608
  6.5 25.1 %slice-start.1 = ((s8[11075584]{0:T(1024)(128)(4,1)}), s8[4194304]{0:T(1024)(128)(4,1)S(1)}, s32[]{:S(2)}) async-start(s8[11075584]{0:T(1024)(128)(4,1)} %bitcast.2), calls=%async_computation.2 | async-start | bytes 8388608
  12.4 19.2 %slice-start.2 = ((s8[11075584]{0:T(1024)(128)(4,1)}), s8[2686976]{0:T(1024)(128)(4,1)S(1)}, s32[]{:S(2)}) async-start(s8[11075584]{0:T(1024)(128)(4,1)} %bitcast.2), calls=%async_computation.3 | async-start | bytes 5373952
  12.4 16.2 %collective-permute-start = (f32[832,1664]{1,0:T(8,128)}, f32[832,1664]{1,0:T(8,128)}, u32[]{:S(2)}, u32[]{:S(2)}) collective-permute-start(f32[832,1664]{1,0:T(8,128)} %slice.13), channel_id=1, source_target_pairs={{0,1},{1,0}} | collective-permute-start | bytes 16613384 | tf_op jit(solution)/shard_map/ppermute | solution.py:363
  21.9 12.7 %copy-start = (s32[32,13]{0,1:T(8,128)S(1)}, s32[32,13]{0,1:T(8,128)}, u32[]{:S(2)}) copy-start(s32[32,13]{0,1:T(8,128)} %param.8) | copy-start | bytes 4996
  21.9 12.7 %collective-permute-start.1 = (bf16[2048,1664]{1,0:T(8,128)(2,1)}, bf16[2048,1664]{1,0:T(8,128)(2,1)}, u32[]{:S(2)}, u32[]{:S(2)}) collective-permute-start(bf16[2048,1664]{1,0:T(8,128)(2,1)} %slice.14), channel_id=1, source_target_pairs={{0,2},{1,3}} | collective-permute-start | bytes 20447240 | tf_op jit(solution)/shard_map/ppermute | solution.py:363
  25.5 9.1 %collective-permute-start.2 = (f32[832,1664]{1,0:T(8,128)}, f32[832,1664]{1,0:T(8,128)}, u32[]{:S(2)}, u32[]{:S(2)}) collective-permute-start(f32[832,1664]{1,0:T(8,128)} %slice.13), channel_id=1, source_target_pairs={{0,2},{1,3}} | collective-permute-start | bytes 16613384 | tf_op jit(solution)/shard_map/ppermute | solution.py:363
  28.6 6.0 %collective-permute-start.3 = (f32[832,1664]{1,0:T(8,128)}, f32[832,1664]{1,0:T(8,128)}, u32[]{:S(2)}, u32[]{:S(2)}) collective-permute-start(f32[832,1664]{1,0:T(8,128)} %collective-permute-done), channel_id=1, source_target_pairs={{0,2},{1,3}} | collective-permute-start | bytes 16613384 | tf_op jit(solution)/shard_map/ppermute | solution.py:363
  41.4 248.9 %collective-permute-start.4 = (bf16[2048,1664]{1,0:T(8,128)(2,1)}, bf16[2048,1664]{1,0:T(8,128)(2,1)}, u32[]{:S(2)}, u32[]{:S(2)}) collective-permute-start(bf16[2048,1664]{1,0:T(8,128)(2,1)} %get-tuple-element.43.near_ref), channel_id=1, source_target_pairs={{2,0},{3,1}} | collective-permute-start | bytes 20447240 | tf_op jit(solution)/shard_map/ppermute | solution.py:363
Sparse Core Ops, SparseCore 0:
  34.7 182.0 all-gather.1
where the time goes:
time: 363 us
  Pallas kernels  311 us (86%)
  local copies, waits for them, and re-layouts  18.8 us (5%)
  starting transfers between devices  16.3 us (4%)
  between operations  13.5 us (4%)
    pallas_call x1, Pallas kernels, spread(): pl.pallas_call(partial(spread_kernel, devices // 2, pieces), out_shape=ja...  245 us
    pallas_call x1, Pallas kernels, trail(): pl.pallas_call(trail_kernel, out_shape=jax.ShapeDtypeStruct(weight.shape,...  65.9 us
    ppermute x5, starting transfers between devices, move(): return lax.ppermute(x, ('col', 'row'), pairs)  16.3 us
  transfers between devices with their start and end apart: 6, of which 0 were waited for; matrix products, arithmetic and copies ran while one was open for 4% of the time, Pallas kernels for 68%

commit v1 on v0

--- a/solution.py
+++ b/solution.py
@@ -30,7 +30,7 @@
 
 def prune_kernel(lanes, lane_ref, keep_ref, w_ref, *refs):
     pieces = refs[:lanes]
-    e_ref, kept_ref, f_ref, f_high, f_low, blocks, inv, inv_high, inv_low, e_low, sems = refs[lanes:]
+    e_ref, kept_ref, f_high, band, blocks, inv, inv_high, inv_low, e_low, sems = refs[lanes:]
     chunk, pcols = w_ref.shape
     depth = pcols // lanes
     supers = inv.shape[0]
@@ -42,22 +42,17 @@
         copies = []
         for s in range(lanes):
             place = lax.rem(lane_ref[0] + lanes - s, lanes)
+            rows = pl.ds(pl.multiple_of(place * depth, 16), depth)
             copies.append(
-                pltpu.make_async_copy(
-                    pieces[s],
-                    f_ref.at[pl.ds(pl.multiple_of(place * depth, 8), depth)],
-                    sems.at[s],
-                )
+                pltpu.make_async_copy(pieces[s].at[:, :pcols], f_high.at[rows], sems.at[2 * s])
+            )
+            copies.append(
+                pltpu.make_async_copy(pieces[s].at[:, pcols:], band.at[rows], sems.at[2 * s + 1])
             )
         for copy in copies:
             copy.start()
         for copy in copies:
             copy.wait()
-        for low in range(0, pcols, BLK):
-            rows = slice(low, low + BLK)
-            high_part, low_part = split(f_ref[rows, :])
-            f_high[rows, :] = high_part
-            f_low[rows, :] = low_part
         eye = row_id == col_id
         pair = (row_id // 2 == col_id // 2) & (row_id < col_id)
         for s in range(supers):
@@ -65,7 +60,10 @@
             width = min(SUP, pcols - lo)
             if width < SUP:
                 blocks[s] = jnp.where(eye, 1.0, 0.0)
-            blocks[s, :width, :width] = f_ref[lo : lo + width, lo : lo + width]
+            shift = lo - min(lo, pcols - SUP)
+            blocks[s, :width, :width] = f_high[lo : lo + width, lo : lo + width].astype(
+                jnp.float32
+            ) + band[lo : lo + width, shift : shift + width].astype(jnp.float32)
             block = blocks[s]
             diagonal = jnp.where(eye, block, 0.0)
             per_row = 1.0 / jnp.sum(diagonal, axis=1, keepdims=True)
@@ -101,8 +99,7 @@
         if lo:
             head = e_ref[:, :lo]
             current = current - (
-                mul(head, f_high[:lo, cols])
-                + (mul(head, f_low[:lo, cols]) + mul(e_low[:, :lo], f_high[:lo, cols]))
+                mul(head, f_high[:lo, cols]) + mul(e_low[:, :lo], f_high[:lo, cols])
             )
         drop_rows = []
         for g in range(row_blocks):
@@ -128,7 +125,7 @@
             second = slice(lo + BLK, lo + width)
             c_high, c_low = high_part[:, :BLK], low_part[:, :BLK]
             inner = mul(c_high, f_high[first, second]) + (
-                mul(c_high, f_low[first, second]) + mul(c_low, f_high[first, second])
+                mul(c_high, band[first, BLK:]) + mul(c_low, f_high[first, second])
             )
             kept_ref[:, second] = jnp.where(
                 drop[:, BLK:] > 0.5, 0.0, current[:, BLK:] - inner
@@ -136,7 +133,8 @@
 
 
 def prune(lane, panel, keep_rows, *pieces):
-    rows, pcols = panel.shape
+    rows = keep_rows.shape[0] * BLK
+    pcols = keep_rows.shape[1] * BLK
     chunk = min(rows, 512)
     supers = pl.cdiv(pcols, SUP)
     lanes = len(pieces)
@@ -154,15 +152,14 @@
         + [pl.BlockSpec(memory_space=pl.ANY)] * lanes,
         out_specs=(row_spec, row_spec),
         scratch_shapes=[
-            pltpu.VMEM((pcols, pcols), jnp.float32),
             pltpu.VMEM((pcols, pcols), jnp.bfloat16),
-            pltpu.VMEM((pcols, pcols), jnp.bfloat16),
+            pltpu.VMEM((pcols, SUP), jnp.bfloat16),
             pltpu.VMEM((supers, SUP, SUP), jnp.float32),
             pltpu.VMEM((supers, SUP, SUP), jnp.float32),
             pltpu.VMEM((supers, SUP, SUP), jnp.bfloat16),
             pltpu.VMEM((supers, SUP, SUP), jnp.bfloat16),
             pltpu.VMEM((chunk, pcols), jnp.bfloat16),
-            pltpu.SemaphoreType.DMA((lanes,)),
+            pltpu.SemaphoreType.DMA((2 * lanes,)),
         ],
         compiler_params=pltpu.CompilerParams(vmem_limit_bytes=VMEM_BYTES),
         cost_estimate=pl.CostEstimate(
@@ -174,7 +171,9 @@
     )(lane, keep_rows, panel, *pieces)
 
 
-def spread_kernel(chips, pieces, mine_ref, all_ref, out_send, out_recv, sib_send, sib_recv):
+def spread_kernel(
+    chips, pieces, mine_ref, kept_ref, all_ref, far_ref, out_send, out_recv, sib_send, sib_recv, kept_sems
+):
     index = lax.axis_index("col")
     core = index % 2
     chip = index // 2
@@ -252,6 +251,18 @@
         return carry
 
     lax.fori_loop(0, pieces, pass_on, 0)
+    kept_copy = pltpu.make_async_remote_copy(
+        src_ref=kept_ref,
+        dst_ref=far_ref,
+        send_sem=kept_sems.at[0],
+        recv_sem=kept_sems.at[1],
+        device_id={"col": sibling},
+        device_id_type=pl.DeviceIdType.MESH,
+    )
+
+    @pl.when(index == 1)
+    def _():
+        kept_copy.start()
 
     def finish(t, carry):
         @pl.when(step < chips - 1)
@@ -264,16 +275,27 @@
 
     lax.fori_loop(0, pieces, finish, 0)
 
-
-def spread(errors, devices):
+    @pl.when(index == 1)
+    def _():
+        kept_copy.wait_send()
+
+    @pl.when(index == 0)
+    def _():
+        kept_copy.wait_recv()
+
+
+def spread(errors, kept, devices):
     half, pcols = errors.shape
     pieces = half // 64
     return pl.pallas_call(
         partial(spread_kernel, devices // 2, pieces),
-        out_shape=jax.ShapeDtypeStruct((2 * half, pcols), jnp.bfloat16),
-        in_specs=[pl.BlockSpec(memory_space=pltpu.VMEM)],
-        out_specs=pl.BlockSpec(memory_space=pltpu.VMEM),
-        scratch_shapes=[pltpu.SemaphoreType.DMA((pieces,))] * 4,
+        out_shape=(
+            jax.ShapeDtypeStruct((2 * half, pcols), jnp.bfloat16),
+            jax.ShapeDtypeStruct((half, pcols), jnp.bfloat16),
+        ),
+        in_specs=[pl.BlockSpec(memory_space=pltpu.VMEM)] * 2,
+        out_specs=(pl.BlockSpec(memory_space=pltpu.VMEM),) * 2,
+        scratch_shapes=[pltpu.SemaphoreType.DMA((pieces,))] * 4 + [pltpu.SemaphoreType.DMA((2,))],
         compiler_params=pltpu.CompilerParams(
             collective_id=0, has_side_effects=True, vmem_limit_bytes=VMEM_BYTES
         ),
@@ -281,7 +303,7 @@
             flops=0, bytes_accessed=16 * half * pcols, transcendentals=0
         ),
         name="spread_errors",
-    )(errors)
+    )(errors, kept)
 
 
 def trail_kernel(owner_ref, e_ref, f_ref, w_ref, near_ref, far_ref, out_ref):
@@ -363,12 +385,18 @@
         return lax.ppermute(x, ("col", "row"), pairs)
 
     own = factor[:, :pcols]
-    panel = weight[:, :pcols]
+    rounded = lax.reduce_precision(own, 8, 7)
+    remainder = (own - rounded).astype(jnp.bfloat16)
+    super_of = ((lane * depth + jnp.arange(depth, dtype=jnp.int32)) // SUP)[:, None]
+    band = remainder[:, :SUP]
+    for low in range(SUP, pcols, SUP):
+        start = min(low, pcols - SUP)
+        band = jnp.where(super_of == low // SUP, remainder[:, start : start + SUP], band)
+    own = jnp.concatenate([rounded.astype(jnp.bfloat16), band], axis=1)
     received = [own] + [
         move(own, [(r, (r + s) % rows_n) for r in range(rows_n)]) for s in range(1, rows_n)
     ]
-    near_panel, far_panel = panel[:half], panel[half:]
-    far_panel = move(far_panel, to_core)
+    far_panel = move(weight[half:, :pcols], to_core)
     relayed = [move(x, to_core) for x in received]
     near_keep, far_keep = jnp.split(keep_mask, 2, axis=0)
     place = lane.astype(jnp.int32).reshape(1)
@@ -389,13 +417,12 @@
     errors, kept = lax.switch(
         jnp.minimum(section, 2),
         [near_case, far_case, blank],
-        near_panel,
+        weight,
         far_panel,
         received,
         relayed,
     )
-    far_kept = move(kept, [(rows_n + r, r) for r in range(rows_n)])
-    arrived = spread(errors, cols_n)
+    arrived, far_kept = spread(errors, kept, cols_n)
     owner = (section == 0).astype(jnp.int32).reshape(1)
     return trail(owner, arrived, factor_low, weight, kept, far_kept)
 

time: 363 us -> 332 us (0.915)
  Pallas kernels: 311 us -> 286 us
  starting transfers between devices: 16.3 us -> 9.21 us
  other arithmetic: 2.93 us -> 9.62 us
  local copies, waits for them, and re-layouts: 18.8 us -> 13.1 us
    pallas_call x1, Pallas kernels: 245 us -> 220 us  [spread(): pl.pallas_call(partial(spread_kernel, devices // 2, pieces), out_shape=(j...]
    ppermute x5 -> x4, starting transfers between devices: 16.3 us -> 9.21 us  [move(): return lax.ppermute(x, ('col', 'row'), pairs)]
    slice x2 -> x1, local copies, waits for them, and re-layouts: 12.2 us -> 6.31 us  [per_device(): far_panel = move(weight[half:, :pcols], to_core)]
  transfers between devices with their start and end apart: 6 -> 5, of which waited for: 0 -> 0; matrix products, arithmetic and copies ran while one was open for 4% -> 5% of each run, Pallas kernels for 68% -> 66%
where the time goes in v1:
time: 332 us
  Pallas kernels  286 us (86%)
  between operations  13.5 us (4%)
  local copies, waits for them, and re-layouts  13.1 us (4%)
  other arithmetic  9.62 us (3%)
  starting transfers between devices  9.21 us (3%)
    pallas_call x1, Pallas kernels, spread(): pl.pallas_call(partial(spread_kernel, devices // 2, pieces), out_shape=(j...  220 us
    pallas_call x1, Pallas kernels, trail(): pl.pallas_call(trail_kernel, out_shape=jax.ShapeDtypeStruct(weight.shape,...  65.7 us
    ppermute x4, starting transfers between devices, move(): return lax.ppermute(x, ('col', 'row'), pairs)  9.21 us
    another operation x2, local copies, waits for them, and re-layouts  6.73 us
  transfers between devices with their start and end apart: 5, of which 0 were waited for; matrix products, arithmetic and copies ran while one was open for 5% of the time, Pallas kernels for 66%

profile of v1, /device:TPU:13, one launch (start us, length us, event | category | flops | bytes accessed | tf_op | source)
XLA Modules:
  0.0 331.5 jit_solution(17144768701459090778)
XLA Ops:
  6.6 0.0 slice-start
  6.6 0.0 slice-start.1
  6.6 3.5 %reduce-precision_convert_fusion = (bf16[832,1664]{1,0:T(8,128)(2,1)S(1)}, bf16[832,1664]{1,0:T(8,128)(2,1)S(1)}) fusion(f32[832,3328]{1,0:T(8,128)} %param.7), kind=kLoop, calls=%fused_computation.1 | loop fusion | flops 5537792 | bytes 11075584 | tf_op jit(solution)/shard_map/convert_element_type | solution.py:395
  10.1 0.0 slice-start.2
  10.1 1.2 fusion.5
  11.3 2.0 pad_maximum_fusion
  13.3 2.4 collective-permute-start
  15.7 3.0 convert_element_type.12
  18.7 0.0 collective-permute-done
  18.7 0.0 all-gather.2.cloned.1.call-update
  18.7 0.0 copy-start
  18.7 6.3 %slice.35 = bf16[2048,1664]{1,0:T(8,128)(2,1)} slice(bf16[4096,3328]{1,0:T(8,128)(2,1)} %w_ref.1), slice={[2048:4096], [0:1664]} | slice | bytes 13631488 | tf_op jit(solution)/shard_map/slice | solution.py:399
  25.0 3.5 %collective-permute-start.1 = (bf16[2048,1664]{1,0:T(8,128)(2,1)}, bf16[2048,1664]{1,0:T(8,128)(2,1)}, u32[]{:S(2)}, u32[]{:S(2)}) collective-permute-start(bf16[2048,1664]{1,0:T(8,128)(2,1)} %slice.35), channel_id=1, source_target_pairs={{0,2},{1,3}} | collective-permute-start | bytes 20447240 | tf_op jit(solution)/shard_map/ppermute | solution.py:385
  28.5 0.9 collective-permute-start.2
  29.4 2.4 collective-permute-start.3
  31.8 0.0 collective-permute-done.2
  31.8 0.0 collective-permute-done.3
  31.8 0.0 collective-permute-done.1
  31.8 6.9 %conditional.1 = ((bf16[2048,1664]{1,0:T(8,128)(2,1)}, bf16[2048,1664]{1,0:T(8,128)(2,1)})) conditional(s32[]{:T(128)} %clamp.3, (s32[32,13]{0,1:T(8,128)S(1)}, s32[1]{0:T(128)}, bf16[4096,3328]{1,0:T(8,128)(2,1)}, bf16[832,1920]{1,0:T(8,128)(2,1)}, bf16[832,1920]{1,0:T(8,128)(2,1)}) %tuple.34, (s32[32,13]{0,1:T(8,128)S(1)}, ...), branch_computations={%region_0.1_spmd, %region_1.2_spmd, %region_2.3_spmd} | conditional | flops 34024194048 | bytes 31527816 | solution.py:417
  32.0 3.4 %broadcast.178.clone = bf16[2048,1664]{1,0:T(8,128)(2,1)} broadcast(bf16[]{:T(256)} %constant.14.clone), dimensions={} | broadcast | bytes 6815746 | tf_op jit(solution)/shard_map/broadcast.1
  35.4 3.4 %broadcast.178 = bf16[2048,1664]{1,0:T(8,128)(2,1)} broadcast(bf16[]{:T(256)} %constant.14.clone), dimensions={} | broadcast | bytes 6815746 | tf_op jit(solution)/shard_map/broadcast.1
  38.8 220.2 %spread_errors.1 = (bf16[4096,1664]{1,0:T(8,128)(2,1)}, bf16[2048,1664]{1,0:T(8,128)(2,1)}) custom-call(bf16[2048,1664]{1,0:T(8,128)(2,1)} %get-tuple-element.42.mine_ref, bf16[2048,1664]{1,0:T(8,128)(2,1)} %get-tuple-element.43.kept_ref.near_ref), custom_call_target="tpu_custom_call" | custom-call | bytes 54525952 | tf_op jit(solution)/shard_map/spread_errors/pallas_call | solution.py:290
  258.9 0.0 all-gather.2.cloned.1.call-done.f_ref
  259.0 65.7 %compensate_later.1 = bf16[4096,3328]{1,0:T(8,128)(2,1)} custom-call(s32[1]{0:T(128)} %bitcast.owner_ref, bf16[4096,1664]{1,0:T(8,128)(2,1)} %get-tuple-element.44.e_ref, bf16[1664,3328]{1,0:T(8,128)(2,1)} %all-gather.2.cloned.1.call-done.f_ref, bf16[4096,3328]{1,0:T(8,128)(2,1)} %w_ref.1, bf16[2048,1664]{1,0:T(8,128)(2,1)} %get-tuple-element.43.kept_ref.near_ref, ...), custom_call_target="tpu_custom_call" | custom-call | flops 45365592064 | bytes 65601536 | tf_op jit(solution)/shard_map/compensate_later/pallas_call | solution.py:344
  (9 shorter events, 0.1 us)
Async XLA Ops:
  6.5 252.4 %all-gather.2.cloned.1.call-start = ((), (), s32[]{:S(2)}) async-start(), calls=%async_computation | async-start | bytes 16613376 | tf_op jit(solution)/shard_map/all_gather | solution.py:405
  6.6 9.1 %slice-start = ((s8[11075584]{0:T(1024)(128)(4,1)}), s8[4194304]{0:T(1024)(128)(4,1)S(1)}, s32[]{:S(2)}) async-start(s8[11075584]{0:T(1024)(128)(4,1)} %bitcast.2), calls=%async_computation.1 | async-start | bytes 8388608
  6.6 9.1 %slice-start.1 = ((s8[11075584]{0:T(1024)(128)(4,1)}), s8[4194304]{0:T(1024)(128)(4,1)S(1)}, s32[]{:S(2)}) async-start(s8[11075584]{0:T(1024)(128)(4,1)} %bitcast.2), calls=%async_computation.2 | async-start | bytes 8388608
  10.1 5.6 %slice-start.2 = ((s8[11075584]{0:T(1024)(128)(4,1)}), s8[2686976]{0:T(1024)(128)(4,1)S(1)}, s32[]{:S(2)}) async-start(s8[11075584]{0:T(1024)(128)(4,1)} %bitcast.2), calls=%async_computation.3 | async-start | bytes 5373952
  13.3 5.4 %collective-permute-start = (bf16[832,1920]{1,0:T(8,128)(2,1)}, bf16[832,1920]{1,0:T(8,128)(2,1)}, u32[]{:S(2)}, u32[]{:S(2)}) collective-permute-start(bf16[832,1920]{1,0:T(8,128)(2,1)} %pad_maximum_fusion), channel_id=1, source_target_pairs={{0,1},{1,0}} | collective-permute-start | bytes 9584648 | tf_op jit(solution)/shard_map/ppermute | solution.py:385
  18.7 13.1 %copy-start = (s32[32,13]{0,1:T(8,128)S(1)}, s32[32,13]{0,1:T(8,128)}, u32[]{:S(2)}) copy-start(s32[32,13]{0,1:T(8,128)} %param.8) | copy-start | bytes 4996
  25.0 6.8 %collective-permute-start.1 = (bf16[2048,1664]{1,0:T(8,128)(2,1)}, bf16[2048,1664]{1,0:T(8,128)(2,1)}, u32[]{:S(2)}, u32[]{:S(2)}) collective-permute-start(bf16[2048,1664]{1,0:T(8,128)(2,1)} %slice.35), channel_id=1, source_target_pairs={{0,2},{1,3}} | collective-permute-start | bytes 20447240 | tf_op jit(solution)/shard_map/ppermute | solution.py:385
  28.5 3.3 collective-permute-start.2
  29.4 2.4 collective-permute-start.3
Sparse Core Ops, SparseCore 0:
  18.8 166.8 all-gather.1
